TPU v7x, 256 devices: a whole 4x4x8 slice. The times are simulated.
256 devices in a mesh: paper: 32 (over x_lo, z, core), type: 8 (over y, x_hi).
Axes of the slice: x: 4 (x_hi: 2, x_lo: 2; x = x_hi * 2 + x_lo), y: 4, z: 8, core: 2. Of those that a mesh axis runs over, the one named last changes fastest.
Arguments:
- papers: bfloat16 [131072, 512], P(('paper', 'type')), may hold values from -6 to 6
- cited_rows: bfloat16 [4096, 512], P('paper'), may hold values from -6 to 6
- entities: bfloat16 [1024, 512], P('type'), may hold values from -6 to 6
- entity_kinds: int32 [1024], P('type'), may hold values from 0 to 1
- query_weight: bfloat16 [512, 512], replicated, may hold values from -0.25 to 0.25
- key_weight: bfloat16 [3, 512, 512], replicated, may hold values from -0.25 to 0.25
- value_weight: bfloat16 [3, 512, 512], replicated, may hold values from -0.25 to 0.25
- attention_rel: bfloat16 [4, 8, 64, 64], replicated, may hold values from -0.75 to 0.75
- message_rel: bfloat16 [4, 8, 64, 64], replicated, may hold values from -0.75 to 0.75
- relation_prior: float32 [4, 8], replicated, may hold values from 0.5 to 2.5
- output_weight: bfloat16 [512, 512], replicated, may hold values from -0.25 to 0.25
- skip_gate: float32 [1], replicated, may hold values from -1 to 1
- norm_gain: float32 [512], replicated, may hold values from 0.5 to 1.5
- cite_pattern: int32 [1024, 8, 128, 128], P(('paper', 'type')), may hold values from 0 to 1, as said below
- cite_tiles: int32 [1024, 8], P(('paper', 'type')), may hold values from 0 to 31, as said below
- cite_counts: int32 [1024, 8], P(('paper', 'type')), may hold values from 0 to 16384, as said below
- entity_pattern: int32 [1024, 2, 128, 128], P(('paper', 'type')), may hold values from 0 to 1, as said below
- entity_tiles: int32 [1024, 2], P(('paper', 'type')), may hold values from 0 to 7, as said below
- entity_counts: int32 [1024, 2], P(('paper', 'type')), may hold values from 0 to 16384, as said below
Outputs:
- updated: bfloat16 [131072, 512], P(('paper', 'type'))
Inputs may be any that keep to these rules, and one draw needn't show every extreme that they name: `cite_pattern`: entry [a, k, p, c] is 1 where paper 128 * a + p has an edge from source 128 * cite_tiles[a, k] + c, else 0. A tile of papers uses its first 8, 4, 2 or 1 slots (at least one), the same number for all tiles of one device's papers; later slots are all zero. `cite_tiles`: the slots of one tile name distinct tiles. `cite_counts`: the number of ones in the slot's block. `entity_pattern`: as cite_pattern, with sources 128 * entity_tiles[a, k] + c; a tile uses its first 1 to 2 slots, later slots are all zero. `entity_tiles`: the slots of one tile name distinct tiles. `entity_counts`: the number of ones in the slot's block.
All inputs are finite; a program needn't handle non-finite values.
Results may differ from a plain program's by a relative error of at most 0.0087.
Values may be sent and summed in bfloat16 or wider, within the bound.
No kernel may reach another device: no remote copies, remote signals or barrier semaphores. Data moves between devices by JAX's collectives and lax.ppermute only.
A program may use at most 128 MiB of HBM per device.

v0:
```python
import math
import jax
import jax.numpy as jnp
from jax import lax
from jax.sharding import PartitionSpec as P

CAP = 20.0


def head_split(matrix, head_count):
    return matrix.reshape(matrix.shape[0], head_count, matrix.shape[1] // head_count)


def relate(raw_rows, weight):
    head_count = weight.shape[0]
    mapped = jnp.einsum(
        "nhd,hde->nhe", head_split(raw_rows, head_count), weight, preferred_element_type=jnp.float32
    )
    return mapped.reshape(raw_rows.shape)


def project(source_rows, weight):
    return jnp.dot(source_rows, weight, preferred_element_type=jnp.float32).astype(jnp.bfloat16)


def cited_pairs(source_rows, key_weight, value_weight, attention_rel, message_rel):
    key_rows = relate(project(source_rows, key_weight[0]), attention_rel[0]).astype(jnp.bfloat16)
    value_rows = relate(project(source_rows, value_weight[0]), message_rel[0]).astype(jnp.bfloat16)
    return (key_rows, value_rows)


def entity_side(source_rows, kind_ids, key_weight, value_weight, attention_rel, message_rel):
    author = (kind_ids == 0)[:, None]
    key_raw = jnp.where(
        author,
        jnp.dot(source_rows, key_weight[1], preferred_element_type=jnp.float32),
        jnp.dot(source_rows, key_weight[2], preferred_element_type=jnp.float32),
    ).astype(jnp.bfloat16)
    value_raw = jnp.where(
        author,
        jnp.dot(source_rows, value_weight[1], preferred_element_type=jnp.float32),
        jnp.dot(source_rows, value_weight[2], preferred_element_type=jnp.float32),
    ).astype(jnp.bfloat16)
    key_rows = jnp.where(
        author, relate(key_raw, attention_rel[1]), relate(key_raw, attention_rel[2])
    ).astype(jnp.bfloat16)
    value_rows = jnp.where(
        author, relate(value_raw, message_rel[1]), relate(value_raw, message_rel[2])
    ).astype(jnp.bfloat16)
    return (key_rows, value_rows)


def kind_scales(kind_ids, relation_prior, inv_root):
    author = (kind_ids == 0)[:, None]
    return jnp.where(author, relation_prior[1][None, :], relation_prior[2][None, :]) * inv_root


def own_term(query_heads, own_key, own_value, scale):
    head_count = query_heads.shape[1]
    own_dot = jnp.sum(
        query_heads.astype(jnp.float32) * head_split(own_key, head_count).astype(jnp.float32),
        axis=2,
    )
    weights = jnp.exp(CAP * jnp.tanh(own_dot * scale / CAP))
    rounded = lax.optimization_barrier(weights.astype(jnp.bfloat16)).astype(jnp.float32)
    return (rounded[:, :, None] * head_split(own_value, head_count).astype(jnp.float32), weights)


def dense_live(pattern, tile_ids, counts, source_count):
    chosen = (tile_ids[:, :, None] == jnp.arange(source_count, dtype=jnp.int32)[None, None, :]) & (
        counts[:, :, None] > 0
    )
    spread = jnp.einsum(
        "ikj,ikac->iajc",
        chosen.astype(jnp.bfloat16),
        pattern.astype(jnp.bfloat16),
        preferred_element_type=jnp.float32,
    )
    return (
        spread.reshape(pattern.shape[0] * pattern.shape[2], source_count * pattern.shape[3]) > 0.5
    )


def attend(running, query_heads, key_rows, value_rows, scales, live_mask):
    head_count = query_heads.shape[1]
    products = jnp.einsum(
        "thd,shd->hts",
        query_heads,
        head_split(key_rows, head_count),
        preferred_element_type=jnp.float32,
    )
    scores = products * scales.T[:, None, :]
    scores = CAP * jnp.tanh(scores / CAP)
    weights = jnp.where(live_mask[None, :, :], jnp.exp(scores), 0.0)
    numerator, denominator = running
    numerator = numerator + jnp.einsum(
        "hts,shd->thd",
        weights.astype(jnp.bfloat16),
        head_split(value_rows, head_count),
        preferred_element_type=jnp.float32,
    )
    denominator = denominator + jnp.sum(weights, axis=2).T
    return (numerator, denominator)


def sweep_dense(running, query_heads, key_rows, value_rows, scales, live_mask):
    row_count = key_rows.shape[0]
    block_rows = math.gcd(row_count, 512)
    block_count = row_count // block_rows

    def single_block(offset, state):
        part_keys = lax.dynamic_slice_in_dim(key_rows, offset, block_rows, 0)
        part_values = lax.dynamic_slice_in_dim(value_rows, offset, block_rows, 0)
        part_scales = lax.dynamic_slice_in_dim(scales, offset, block_rows, 0)
        part_live = lax.dynamic_slice_in_dim(live_mask, offset, block_rows, 1)
        return attend(state, query_heads, part_keys, part_values, part_scales, part_live)

    return lax.fori_loop(
        0, block_count, lambda position, state: single_block(position * block_rows, state), running
    )


def per_device(
    papers,
    cited_rows,
    entities,
    entity_kinds,
    query_weight,
    key_weight,
    value_weight,
    attention_rel,
    message_rel,
    relation_prior,
    output_weight,
    skip_gate,
    norm_gain,
    cite_pattern,
    cite_tiles,
    cite_counts,
    entity_pattern,
    entity_tiles,
    entity_counts,
):
    head_count = relation_prior.shape[1]
    model_width = papers.shape[1]
    inv_root = 1.0 / math.sqrt(model_width // head_count)
    tile_size = cite_pattern.shape[2]
    query_heads = head_split(project(papers, query_weight), head_count)
    own_keys = relate(project(papers, key_weight[0]), attention_rel[3]).astype(jnp.bfloat16)
    own_values = relate(project(papers, value_weight[0]), message_rel[3]).astype(jnp.bfloat16)
    running = own_term(query_heads, own_keys, own_values, relation_prior[3] * inv_root)
    cite_sources = cited_rows.shape[0] * lax.axis_size("paper") // tile_size
    entity_sources = entities.shape[0] * lax.axis_size("type") // tile_size
    cite_live = dense_live(cite_pattern, cite_tiles, cite_counts, cite_sources)
    entity_live = dense_live(entity_pattern, entity_tiles, entity_counts, entity_sources)
    cite_scale = relation_prior[0] * inv_root

    def sweep_rows(state, key_rows, value_rows, scales, live_mask):
        return sweep_dense(state, query_heads, key_rows, value_rows, scales, live_mask)

    cite_keys, cite_values = cited_pairs(
        cited_rows, key_weight, value_weight, attention_rel, message_rel
    )
    key_rows = lax.all_gather(cite_keys, "paper", axis=0, tiled=True)
    value_rows = lax.all_gather(cite_values, "paper", axis=0, tiled=True)
    row_count = key_rows.shape[0]
    scales = jnp.broadcast_to(cite_scale[None, :], (row_count, head_count))
    live_mask = cite_live
    running = sweep_rows(running, key_rows, value_rows, scales, live_mask)
    entity_keys, entity_values = entity_side(
        entities, entity_kinds, key_weight, value_weight, attention_rel, message_rel
    )
    key_rows = lax.all_gather(entity_keys, "type", axis=0, tiled=True)
    value_rows = lax.all_gather(entity_values, "type", axis=0, tiled=True)
    kind_ids = lax.all_gather(entity_kinds, "type", axis=0, tiled=True)
    live_mask = entity_live
    scales = kind_scales(kind_ids, relation_prior, inv_root)
    running = sweep_rows(running, key_rows, value_rows, scales, live_mask)
    numerator, denominator = running
    mixed = numerator / denominator[:, :, None]
    hidden = jax.nn.gelu(mixed, approximate=False).reshape(papers.shape).astype(jnp.bfloat16)
    projected = jnp.dot(hidden, output_weight, preferred_element_type=jnp.float32)
    alpha = jax.nn.sigmoid(skip_gate[0])
    blended = alpha * projected + (1.0 - alpha) * papers.astype(jnp.float32)
    centre = jnp.mean(blended, axis=1, keepdims=True)
    spread = jnp.mean(jnp.square(blended - centre), axis=1, keepdims=True)
    return ((blended - centre) * lax.rsqrt(spread + 1e-05) * norm_gain).astype(jnp.bfloat16)


def solution(mesh):
    in_specs = (
        P(("paper", "type"), None),
        P("paper", None),
        P("type", None),
        P("type"),
        P(),
        P(),
        P(),
        P(),
        P(),
        P(),
        P(),
        P(),
        P(),
        P(("paper", "type"), None, None, None),
        P(("paper", "type"), None),
        P(("paper", "type"), None),
        P(("paper", "type"), None, None, None),
        P(("paper", "type"), None),
        P(("paper", "type"), None),
    )
    out_specs = P(("paper", "type"), None)
    return jax.shard_map(
        per_device, mesh=mesh, in_specs=in_specs, out_specs=out_specs, check_vma=False
    )
```

profile of v0, /device:TPU:32, one launch (start us, length us, event | category | flops | bytes accessed | tf_op | source)
XLA Modules:
  0.0 305.5 jit_solution(12606027069432902656)
XLA Ops:
  6.5 1.4 convolution_convert_fusion.6
  8.1 1.8 convolution_convert_fusion.8
  10.0 1.5 convolution_convert_fusion.5
  11.6 1.8 convolution_convert_fusion.7
  14.1 1.3 fusion.50
  15.4 1.4 fusion.37
  16.9 1.1 fusion.68
  18.8 1.3 fusion.53
  20.2 1.4 fusion.36
  21.7 1.1 fusion.74
  23.6 1.1 fusion.72
  25.5 1.1 fusion.70
  26.8 1.8 select_convert_fusion
  29.2 2.3 convolution_convert_fusion.3
  31.5 2.4 convolution_convert_fusion.2
  34.9 1.5 convolution_convert_fusion.4
  36.5 1.6 fusion.35
  39.2 2.5 broadcast_compare_fusion
  41.7 3.0 copy.131
  44.7 23.5 %all-gather = s32[8,1,128]{2,1,0:T(1,128)S(1)} all-gather(s32[1,1,128]{2,1,0:T(1,128)S(1)} %bitcast.259), channel_id=1, replica_groups=mesh['paper'=32,'type'=8] {'type'}, dimensions={0}, use_global_device_ids=true | all-gather | bytes 4608 | tf_op jit(solution)/shard_map/all_gather | solution.py:175
  70.2 2.3 fusion.34
  72.5 12.5 %all-gather.6.cloned.1.call-done = bf16[4096,512]{0,1:T(8,128)(2,1)} async-done(((bf16[128,512]{0,1:T(8,128)(2,1)}), bf16[4096,512]{0,1:T(8,128)(2,1)}) %all-gather.6.cloned.1.call-update) | async-done | bytes 4194320 | tf_op jit(solution)/shard_map/all_gather | solution.py:165
  85.0 72.5 %all-gather.8.cloned.1.call-done = bf16[4096,512]{0,1:T(8,128)(2,1)} async-done(((bf16[128,512]{0,1:T(8,128)(2,1)}), bf16[4096,512]{0,1:T(8,128)(2,1)}) %all-gather.8.cloned.1.call-update) | async-done | bytes 4194320 | tf_op jit(solution)/shard_map/all_gather | solution.py:164
  158.3 92.3 %while.30 = (s32[]{:T(128)}, f32[512,8,64]{0,2,1:T(8,128)}, f32[512,8]{0,1:T(8,128)S(1)}, bf16[4096,512]{0,1:T(8,128)(2,1)}, pred[512,4096]{1,0:T(8,128)(4,1)}, ...) while((s32[]{:T(128)}, f32[512,8,64]{0,2,1:T(8,128)}, ...), condition=%wide.region_3.4_spmd, body=%wide.region_1.3_spmd.sunk | while | flops 558104576 | bytes 32637160 | solution.py:118
  158.3 1.3 constant_dynamic-slice_fusion.10
  161.6 4.5 %fusion.143 = (f32[8,512]{1,0:T(8,128)S(1)}, f32[8,512,512]{2,1,0:T(8,128)S(1)}) fusion(f32[8,512]{1,0:T(8,128)S(1)} %dynamic-slice_bitcast_fusion.4, pred[512,512]{0,1:T(8,128)(4,1)S(1)} %copy.137, bf16[512,8,64]{0,2,1:T(8,128)(2,1)S(1)} %bitcast.234, bf16[512,8,64]{0,2,1:T(8,128)(2,1)} %get-tuple-element.531), kind=kOutput, calls=%fused_computation.1.clone.1 | convolution fusion | flops 278917120 | bytes 9732096 | tf_op jit(solution)/shard_map/while/body/eval_jaxpr/thd,shd->hts/dot_general | solution.py:86
  166.1 2.6 fusion.144
  168.8 1.0 copy-done.2
  169.8 1.3 constant_dynamic-slice_fusion.10
  173.2 4.5 %fusion.143 = (f32[8,512]{1,0:T(8,128)S(1)}, f32[8,512,512]{2,1,0:T(8,128)S(1)}) fusion(f32[8,512]{1,0:T(8,128)S(1)} %dynamic-slice_bitcast_fusion.4, pred[512,512]{0,1:T(8,128)(4,1)S(1)} %copy.137, bf16[512,8,64]{0,2,1:T(8,128)(2,1)S(1)} %bitcast.234, bf16[512,8,64]{0,2,1:T(8,128)(2,1)} %get-tuple-element.531), kind=kOutput, calls=%fused_computation.1.clone.1 | convolution fusion | flops 278917120 | bytes 9732096 | tf_op jit(solution)/shard_map/while/body/eval_jaxpr/thd,shd->hts/dot_general | solution.py:86
  177.7 2.6 fusion.144
  180.4 1.0 copy-done.2
  181.4 1.3 constant_dynamic-slice_fusion.10
  184.8 4.5 %fusion.143 = (f32[8,512]{1,0:T(8,128)S(1)}, f32[8,512,512]{2,1,0:T(8,128)S(1)}) fusion(f32[8,512]{1,0:T(8,128)S(1)} %dynamic-slice_bitcast_fusion.4, pred[512,512]{0,1:T(8,128)(4,1)S(1)} %copy.137, bf16[512,8,64]{0,2,1:T(8,128)(2,1)S(1)} %bitcast.234, bf16[512,8,64]{0,2,1:T(8,128)(2,1)} %get-tuple-element.531), kind=kOutput, calls=%fused_computation.1.clone.1 | convolution fusion | flops 278917120 | bytes 9732096 | tf_op jit(solution)/shard_map/while/body/eval_jaxpr/thd,shd->hts/dot_general | solution.py:86
  189.2 2.6 fusion.144
  191.9 1.0 copy-done.2
  192.9 1.3 constant_dynamic-slice_fusion.10
  196.3 4.5 %fusion.143 = (f32[8,512]{1,0:T(8,128)S(1)}, f32[8,512,512]{2,1,0:T(8,128)S(1)}) fusion(f32[8,512]{1,0:T(8,128)S(1)} %dynamic-slice_bitcast_fusion.4, pred[512,512]{0,1:T(8,128)(4,1)S(1)} %copy.137, bf16[512,8,64]{0,2,1:T(8,128)(2,1)S(1)} %bitcast.234, bf16[512,8,64]{0,2,1:T(8,128)(2,1)} %get-tuple-element.531), kind=kOutput, calls=%fused_computation.1.clone.1 | convolution fusion | flops 278917120 | bytes 9732096 | tf_op jit(solution)/shard_map/while/body/eval_jaxpr/thd,shd->hts/dot_general | solution.py:86
  200.8 2.6 fusion.144
  203.4 1.0 copy-done.2
  204.4 1.3 constant_dynamic-slice_fusion.10
  207.8 4.5 %fusion.143 = (f32[8,512]{1,0:T(8,128)S(1)}, f32[8,512,512]{2,1,0:T(8,128)S(1)}) fusion(f32[8,512]{1,0:T(8,128)S(1)} %dynamic-slice_bitcast_fusion.4, pred[512,512]{0,1:T(8,128)(4,1)S(1)} %copy.137, bf16[512,8,64]{0,2,1:T(8,128)(2,1)S(1)} %bitcast.234, bf16[512,8,64]{0,2,1:T(8,128)(2,1)} %get-tuple-element.531), kind=kOutput, calls=%fused_computation.1.clone.1 | convolution fusion | flops 278917120 | bytes 9732096 | tf_op jit(solution)/shard_map/while/body/eval_jaxpr/thd,shd->hts/dot_general | solution.py:86
  212.3 2.6 fusion.144
  215.0 1.0 copy-done.2
  216.0 1.3 constant_dynamic-slice_fusion.10
  219.4 4.5 %fusion.143 = (f32[8,512]{1,0:T(8,128)S(1)}, f32[8,512,512]{2,1,0:T(8,128)S(1)}) fusion(f32[8,512]{1,0:T(8,128)S(1)} %dynamic-slice_bitcast_fusion.4, pred[512,512]{0,1:T(8,128)(4,1)S(1)} %copy.137, bf16[512,8,64]{0,2,1:T(8,128)(2,1)S(1)} %bitcast.234, bf16[512,8,64]{0,2,1:T(8,128)(2,1)} %get-tuple-element.531), kind=kOutput, calls=%fused_computation.1.clone.1 | convolution fusion | flops 278917120 | bytes 9732096 | tf_op jit(solution)/shard_map/while/body/eval_jaxpr/thd,shd->hts/dot_general | solution.py:86
  223.8 2.6 fusion.144
  227.5 1.3 constant_dynamic-slice_fusion.10
  230.9 4.5 %fusion.143 = (f32[8,512]{1,0:T(8,128)S(1)}, f32[8,512,512]{2,1,0:T(8,128)S(1)}) fusion(f32[8,512]{1,0:T(8,128)S(1)} %dynamic-slice_bitcast_fusion.4, pred[512,512]{0,1:T(8,128)(4,1)S(1)} %copy.137, bf16[512,8,64]{0,2,1:T(8,128)(2,1)S(1)} %bitcast.234, bf16[512,8,64]{0,2,1:T(8,128)(2,1)} %get-tuple-element.531), kind=kOutput, calls=%fused_computation.1.clone.1 | convolution fusion | flops 278917120 | bytes 9732096 | tf_op jit(solution)/shard_map/while/body/eval_jaxpr/thd,shd->hts/dot_general | solution.py:86
  235.4 2.6 fusion.144
  239.1 1.3 constant_dynamic-slice_fusion.10
  242.4 4.5 %fusion.143 = (f32[8,512]{1,0:T(8,128)S(1)}, f32[8,512,512]{2,1,0:T(8,128)S(1)}) fusion(f32[8,512]{1,0:T(8,128)S(1)} %dynamic-slice_bitcast_fusion.4, pred[512,512]{0,1:T(8,128)(4,1)S(1)} %copy.137, bf16[512,8,64]{0,2,1:T(8,128)(2,1)S(1)} %bitcast.234, bf16[512,8,64]{0,2,1:T(8,128)(2,1)} %get-tuple-element.531), kind=kOutput, calls=%fused_computation.1.clone.1 | convolution fusion | flops 278917120 | bytes 9732096 | tf_op jit(solution)/shard_map/while/body/eval_jaxpr/thd,shd->hts/dot_general | solution.py:86
  246.9 2.6 fusion.144
  250.6 12.6 %all-gather.12.cloned.1.call-done = bf16[1024,512]{1,0:T(8,128)(2,1)} async-done(((bf16[128,512]{1,0:T(8,128)(2,1)}), bf16[1024,512]{1,0:T(8,128)(2,1)}) %all-gather.12.cloned.1.call-update) | async-done | bytes 1048592 | tf_op jit(solution)/shard_map/all_gather | solution.py:173
  263.2 29.5 %while.31 = (s32[]{:T(128)}, f32[512,8,64]{0,2,1:T(8,128)}, f32[512,8]{0,1:T(8,128)S(1)}, bf16[1024,512]{1,0:T(8,128)(2,1)}, pred[512,1024]{1,0:T(8,128)(4,1)S(1...) while((s32[]{:T(128)}, f32[512,8,64]{0,2,1:T(8,128)}, ...), condition=%wide.region_6.7_spmd, body=%wide.region_4.6_spmd.sunk | while | flops 558104576 | bytes 34734312 | solution.py:118
  263.2 1.3 constant_dynamic-slice_fusion.12
  265.1 6.5 %fusion.149 = (f32[8,512]{1,0:T(8,128)S(1)}, f32[8,512,512]{2,1,0:T(8,128)}) fusion(f32[8,512]{1,0:T(8,128)S(1)} %dynamic-slice_bitcast_fusion.5, pred[512,512]{0,1:T(8,128)(4,1)S(1)} %copy.139, bf16[512,8,64]{0,2,1:T(8,128)(2,1)S(1)} %bitcast.235, bf16[512,8,64]{0,2,1:T(8,128)(2,1)} %get-tuple-element.567), kind=kOutput, calls=%fused_computation.16.clone.1 | convolution fusion | flops 278917120 | bytes 9732096 | tf_op jit(solution)/shard_map/while/body/eval_jaxpr/thd,shd->hts/dot_general | solution.py:86
  271.8 5.0 %fusion.150 = f32[512,8,64]{0,2,1:T(8,128)S(1)} fusion(f32[512,8,64]{0,2,1:T(8,128)S(1)} %copy-done.3, bf16[512,8,64]{0,2,1:T(8,128)(2,1)S(1)} %bitcast.236, f32[8,512,512]{2,1,0:T(8,128)} %get-tuple-element.499, f32[8,512]{1,0:T(8,128)S(1)} %dynamic-slice_bitcast_fusion.5, pred[512,512]{0,1:T(8,128)(4,1)S(1)} %copy.139), kind=kOutput, calls=%fused_computation.21.clone.1 | convolution fusion | flops 279183360 | bytes 11288576 | tf_op jit(solution)/shard_map/while/body/eval_jaxpr/hts,shd->thd/dot_general | solution.py:96
  276.9 1.0 copy-done.4
  277.9 1.3 constant_dynamic-slice_fusion.12
  279.9 6.5 %fusion.149 = (f32[8,512]{1,0:T(8,128)S(1)}, f32[8,512,512]{2,1,0:T(8,128)}) fusion(f32[8,512]{1,0:T(8,128)S(1)} %dynamic-slice_bitcast_fusion.5, pred[512,512]{0,1:T(8,128)(4,1)S(1)} %copy.139, bf16[512,8,64]{0,2,1:T(8,128)(2,1)S(1)} %bitcast.235, bf16[512,8,64]{0,2,1:T(8,128)(2,1)} %get-tuple-element.567), kind=kOutput, calls=%fused_computation.16.clone.1 | convolution fusion | flops 278917120 | bytes 9732096 | tf_op jit(solution)/shard_map/while/body/eval_jaxpr/thd,shd->hts/dot_general | solution.py:86
  286.6 5.0 %fusion.150 = f32[512,8,64]{0,2,1:T(8,128)S(1)} fusion(f32[512,8,64]{0,2,1:T(8,128)S(1)} %copy-done.3, bf16[512,8,64]{0,2,1:T(8,128)(2,1)S(1)} %bitcast.236, f32[8,512,512]{2,1,0:T(8,128)} %get-tuple-element.499, f32[8,512]{1,0:T(8,128)S(1)} %dynamic-slice_bitcast_fusion.5, pred[512,512]{0,1:T(8,128)(4,1)S(1)} %copy.139), kind=kOutput, calls=%fused_computation.21.clone.1 | convolution fusion | flops 279183360 | bytes 11288576 | tf_op jit(solution)/shard_map/while/body/eval_jaxpr/hts,shd->thd/dot_general | solution.py:96
  292.6 3.4 %fusion.40 = bf16[512,8,64]{0,2,1:T(8,128)(2,1)S(1)} fusion(f32[512,8,64]{0,2,1:T(8,128)} %get-tuple-element.287, f32[512,8]{0,1:T(8,128)S(1)} %get-tuple-element.288), kind=kLoop, calls=%fused_computation.59 | loop fusion | flops 17301504 | bytes 1589248 | tf_op jit(solution)/shard_map/convert_element_type | solution.py:181
  296.1 1.6 fusion.100
  (138 shorter events, 32.3 us)
Async XLA Ops:
  6.5 289.5 %copy-start = (bf16[512,512]{1,0:T(8,128)(2,1)S(1)}, bf16[512,512]{1,0:T(8,128)(2,1)}, u32[]{:S(2)}) copy-start(bf16[512,512]{1,0:T(8,128)(2,1)} %param.33) | copy-start | bytes 1572868
  6.5 22.7 %copy-start.6 = (bf16[512,512]{1,0:T(8,128)(2,1)S(1)}, bf16[512,512]{1,0:T(8,128)(2,1)}, u32[]{:S(2)}) copy-start(bf16[512,512]{1,0:T(8,128)(2,1)} %param.23) | copy-start | bytes 1572868
  6.5 28.4 %copy-start.11 = (f32[4,8]{1,0:T(4,128)S(1)}, f32[4,8]{1,0:T(4,128)}, u32[]{:S(2)}) copy-start(f32[4,8]{1,0:T(4,128)} %param.32) | copy-start | bytes 388
  6.5 78.5 %all-gather.6.cloned.1.call-start = ((), (), s32[]{:S(2)}) async-start(), calls=%async_computation | async-start | bytes 4325376 | tf_op jit(solution)/shard_map/all_gather | solution.py:165
  9.9 28.3 %copy-start.7 = (s32[4,8,128,128]{3,2,1,0:T(8,128)S(1)}, s32[4,8,128,128]{3,2,1,0:T(8,128)}, u32[]{:S(2)}) copy-start(s32[4,8,128,128]{3,2,1,0:T(8,128)} %param.36) | copy-start | bytes 6291460
  9.9 147.6 %all-gather.8.cloned.1.call-start = ((), (), s32[]{:S(2)}) async-start(), calls=%async_computation.1 | async-start | bytes 4325376 | tf_op jit(solution)/shard_map/all_gather | solution.py:164
  13.4 237.2 %all-gather.10.cloned.1.call-start = ((), (), s32[]{:S(2)}) async-start(), calls=%async_computation.2 | async-start | bytes 1179648 | tf_op jit(solution)/shard_map/all_gather | solution.py:174
  28.6 234.5 %all-gather.12.cloned.1.call-start = ((), (), s32[]{:S(2)}) async-start(), calls=%async_computation.3 | async-start | bytes 1179648 | tf_op jit(solution)/shard_map/all_gather | solution.py:173
  36.5 1.7 copy-start.5
  39.2 5.6 %copy-start.13 = (s32[128]{0:T(128)S(1)}, s32[128]{0:T(128)}, u32[]{:S(2)}) copy-start(s32[128]{0:T(128)} %param.26) | copy-start | bytes 1540
  39.2 29.0 %copy-start.8 = (s32[4,2,128,128]{3,2,1,0:T(8,128)S(1)}, s32[4,2,128,128]{3,2,1,0:T(8,128)}, u32[]{:S(2)}) copy-start(s32[4,2,128,128]{3,2,1,0:T(8,128)} %param.39) | copy-start | bytes 1572868
  39.2 29.1 %copy-start.12 = (s32[4,2]{0,1:T(2,128)S(1)}, s32[4,2]{0,1:T(2,128)}, u32[]{:S(2)}) copy-start(s32[4,2]{0,1:T(2,128)} %param.40) | copy-start | bytes 100
  39.2 29.2 %copy-start.14 = (s32[4,2]{0,1:T(2,128)S(1)}, s32[4,2]{0,1:T(2,128)}, u32[]{:S(2)}) copy-start(s32[4,2]{0,1:T(2,128)} %param.41) | copy-start | bytes 100
  41.7 28.5 %copy-start.9 = (bf16[512,512]{0,1:T(8,128)(2,1)S(1)}, bf16[512,512]{0,1:T(8,128)(2,1)}, u32[]{:S(2)}) copy-start(bf16[512,512]{0,1:T(8,128)(2,1)} %convolution_convert_fusion.2) | copy-start | bytes 1572868
  161.6 4.5 %copy-start.1 = (f32[512,8,64]{0,2,1:T(8,128)S(1)}, f32[512,8,64]{0,2,1:T(8,128)}, u32[]{:S(2)}) copy-start(f32[512,8,64]{0,2,1:T(8,128)} %get-tuple-element.514) | copy-start | bytes 3145732 | tf_op jit(solution)/shard_map/while
  168.8 1.0 copy-start.2
  173.2 4.5 %copy-start.1 = (f32[512,8,64]{0,2,1:T(8,128)S(1)}, f32[512,8,64]{0,2,1:T(8,128)}, u32[]{:S(2)}) copy-start(f32[512,8,64]{0,2,1:T(8,128)} %get-tuple-element.514) | copy-start | bytes 3145732 | tf_op jit(solution)/shard_map/while
  180.3 1.0 copy-start.2
  184.8 4.5 %copy-start.1 = (f32[512,8,64]{0,2,1:T(8,128)S(1)}, f32[512,8,64]{0,2,1:T(8,128)}, u32[]{:S(2)}) copy-start(f32[512,8,64]{0,2,1:T(8,128)} %get-tuple-element.514) | copy-start | bytes 3145732 | tf_op jit(solution)/shard_map/while
  191.9 1.0 copy-start.2
  196.3 4.5 %copy-start.1 = (f32[512,8,64]{0,2,1:T(8,128)S(1)}, f32[512,8,64]{0,2,1:T(8,128)}, u32[]{:S(2)}) copy-start(f32[512,8,64]{0,2,1:T(8,128)} %get-tuple-element.514) | copy-start | bytes 3145732 | tf_op jit(solution)/shard_map/while
  203.4 1.0 copy-start.2
  207.8 4.5 %copy-start.1 = (f32[512,8,64]{0,2,1:T(8,128)S(1)}, f32[512,8,64]{0,2,1:T(8,128)}, u32[]{:S(2)}) copy-start(f32[512,8,64]{0,2,1:T(8,128)} %get-tuple-element.514) | copy-start | bytes 3145732 | tf_op jit(solution)/shard_map/while
  215.0 1.0 copy-start.2
  219.4 4.5 %copy-start.1 = (f32[512,8,64]{0,2,1:T(8,128)S(1)}, f32[512,8,64]{0,2,1:T(8,128)}, u32[]{:S(2)}) copy-start(f32[512,8,64]{0,2,1:T(8,128)} %get-tuple-element.514) | copy-start | bytes 3145732 | tf_op jit(solution)/shard_map/while
  226.5 1.0 copy-start.2
  230.9 4.5 %copy-start.1 = (f32[512,8,64]{0,2,1:T(8,128)S(1)}, f32[512,8,64]{0,2,1:T(8,128)}, u32[]{:S(2)}) copy-start(f32[512,8,64]{0,2,1:T(8,128)} %get-tuple-element.514) | copy-start | bytes 3145732 | tf_op jit(solution)/shard_map/while
  238.0 1.0 copy-start.2
  242.4 4.5 %copy-start.1 = (f32[512,8,64]{0,2,1:T(8,128)S(1)}, f32[512,8,64]{0,2,1:T(8,128)}, u32[]{:S(2)}) copy-start(f32[512,8,64]{0,2,1:T(8,128)} %get-tuple-element.514) | copy-start | bytes 3145732 | tf_op jit(solution)/shard_map/while
  249.6 1.0 copy-start.2
  263.2 34.7 %copy-start.10 = (f32[512]{0:T(512)S(1)}, f32[512]{0:T(512)}, u32[]{:S(2)}) copy-start(f32[512]{0:T(512)} %param.35) | copy-start | bytes 6148
  265.1 6.7 %copy-start.3 = (f32[512,8,64]{0,2,1:T(8,128)S(1)}, f32[512,8,64]{0,2,1:T(8,128)}, u32[]{:S(2)}) copy-start(f32[512,8,64]{0,2,1:T(8,128)} %get-tuple-element.550) | copy-start | bytes 3145732 | tf_op jit(solution)/shard_map/while
  276.9 1.0 copy-start.4
  279.8 6.7 %copy-start.3 = (f32[512,8,64]{0,2,1:T(8,128)S(1)}, f32[512,8,64]{0,2,1:T(8,128)}, u32[]{:S(2)}) copy-start(f32[512,8,64]{0,2,1:T(8,128)} %get-tuple-element.550) | copy-start | bytes 3145732 | tf_op jit(solution)/shard_map/while
  291.6 1.0 copy-start.4
Sparse Core Ops, SparseCore 0:
  10.0 74.9 all-gather.5
  86.8 70.6 all-gather.7
  160.2 50.1 all-gather.9
  212.8 50.2 all-gather.11
where the time goes:
time: 307 us; the launch traced here: 306 us
  matrix products  111 us (36%)
  waiting for transfers between devices  98.1 us (32%)
  local copies, waits for them, and re-layouts  50.6 us (16%)
  blocking collectives  23.5 us (8%)
  between operations  14.1 us (5%)
  other arithmetic  7.42 us (2%)
    all_gather x1, waiting for transfers between devices, per_device(): key_rows = lax.all_gather(cite_keys, 'paper', axis=0, tiled=True)  72.5 us
    dot_general x10, matrix products, attend(): jnp.einsum('thd,shd->hts', query_heads, head_split(key_rows, head_count),...  48.6 us
    dot_general x10, matrix products, attend(): jnp.einsum('hts,shd->thd', weights.astype(jnp.bfloat16), head_split(value...  31.2 us
    all_gather x1, blocking collectives, per_device(): kind_ids = lax.all_gather(entity_kinds, 'type', axis=0, tiled=True)  23.5 us
    dynamic_slice x12, local copies, waits for them, and re-layouts, single_block(): part_keys = lax.dynamic_slice_in_dim(key_rows, offset, block_rows, 0)  13.2 us
    all_gather x1, waiting for transfers between devices, per_device(): key_rows = lax.all_gather(entity_keys, 'type', axis=0, tiled=True)  12.6 us
    all_gather x1, waiting for transfers between devices, per_device(): value_rows = lax.all_gather(cite_values, 'paper', axis=0, tiled=True)  12.5 us
    dot_general x8, matrix products, relate(): jnp.einsum('nhd,hde->nhe', head_split(raw_rows, head_count), weight, pref...  12 us
  transfers between devices with their start and end apart: 4, of which 3 were waited for; matrix products, arithmetic and copies ran while one was open for 40% of the time, Pallas kernels for 0%

commit v1 on v0

--- a/solution.py
+++ b/solution.py
@@ -170,8 +170,13 @@
     entity_keys, entity_values = entity_side(
         entities, entity_kinds, key_weight, value_weight, attention_rel, message_rel
     )
-    key_rows = lax.all_gather(entity_keys, "type", axis=0, tiled=True)
-    value_rows = lax.all_gather(entity_values, "type", axis=0, tiled=True)
+    key_rows, value_rows = jnp.split(
+        lax.all_gather(
+            jnp.concatenate([entity_keys, entity_values], axis=1), "type", axis=0, tiled=True
+        ),
+        [entity_keys.shape[1]],
+        axis=1,
+    )
     kind_ids = lax.all_gather(entity_kinds, "type", axis=0, tiled=True)
     live_mask = entity_live
     scales = kind_scales(kind_ids, relation_prior, inv_root)

time: 307 us -> 356 us (1.16)
  waiting for transfers between devices: 98.1 us -> 156 us
  matrix products: 111 us -> 102 us
    all_gather x1, waiting for transfers between devices: 12.5 us -> 69.1 us  [per_device(): value_rows = lax.all_gather(cite_values, 'paper', axis=0, tiled=True)]
    transpose x10, local copies, waits for them, and re-layouts: 5.83 us -> 0.11 us  [attend(): scores = products * scales.T[:, None, :]]
    dot_general x10, matrix products: 31.2 us -> 26.4 us  [attend(): jnp.einsum('hts,shd->thd', weights.astype(jnp.bfloat16), head_split(value...]
    dot_general x10, matrix products: 48.6 us -> 44.5 us  [attend(): jnp.einsum('thd,shd->hts', query_heads, head_split(key_rows, head_count),...]
    all_gather x2 -> x1, waiting for transfers between devices: 12.6 us -> 14.2 us  [per_device(): lax.all_gather(jnp.concatenate([entity_keys, entity_values], axis=1), 'ty...]
  transfers between devices with their start and end apart: 4 -> 3, of which waited for: 3 -> 3; matrix products, arithmetic and copies ran while one was open for 40% -> 7% of each run, Pallas kernels for 0% -> 0%
where the time goes in v1:
time: 356 us; the launch traced here: 353 us
  waiting for transfers between devices  156 us (44%)
  matrix products  102 us (29%)
  local copies, waits for them, and re-layouts  50.2 us (14%)
  blocking collectives  23.6 us (7%)
  between operations  14.2 us (4%)
  other arithmetic  6.74 us (2%)
    all_gather x1, waiting for transfers between devices, per_device(): key_rows = lax.all_gather(cite_keys, 'paper', axis=0, tiled=True)  72.7 us
    all_gather x1, waiting for transfers between devices, per_device(): value_rows = lax.all_gather(cite_values, 'paper', axis=0, tiled=True)  69.1 us
    dot_general x10, matrix products, attend(): jnp.einsum('thd,shd->hts', query_heads, head_split(key_rows, head_count),...  44.5 us
    dot_general x10, matrix products, attend(): jnp.einsum('hts,shd->thd', weights.astype(jnp.bfloat16), head_split(value...  26.4 us
    all_gather x1, blocking collectives, per_device(): kind_ids = lax.all_gather(entity_kinds, 'type', axis=0, tiled=True)  23.6 us
    all_gather x1, waiting for transfers between devices, per_device(): lax.all_gather(jnp.concatenate([entity_keys, entity_values], axis=1), 'ty...  14.2 us
    dynamic_slice x20, local copies, waits for them, and re-layouts, single_block(): part_live = lax.dynamic_slice_in_dim(live_mask, offset, block_rows, 1)  13.7 us
    dot_general x8, matrix products, relate(): jnp.einsum('nhd,hde->nhe', head_split(raw_rows, head_count), weight, pref...  13.1 us
  transfers between devices with their start and end apart: 3, of which 3 were waited for; matrix products, arithmetic and copies ran while one was open for 7% of the time, Pallas kernels for 0%

profile of v1, /device:TPU:32, one launch (start us, length us, event | category | flops | bytes accessed | tf_op | source)
XLA Modules:
  0.0 353.1 jit_solution(13931623936210666346)
XLA Ops:
  7.3 1.5 fusion.53
  8.8 1.4 fusion.36
  10.3 1.1 fusion.74
  11.4 1.1 fusion.72
  12.5 1.3 fusion.50
  13.9 2.0 fusion.37
  15.9 1.0 copy.93
  17.0 1.8 fusion.70
  18.8 1.8 fusion.68
  20.8 1.0 copy.96
  21.8 1.7 copy.97
  25.3 1.3 convolution_convert_fusion.6
  26.8 1.8 convolution_convert_fusion.8
  28.6 1.3 convolution_convert_fusion.5
  30.1 1.8 convolution_convert_fusion.7
  31.9 1.0 copy.105
  33.7 1.5 convolution_convert_fusion.3
  35.2 1.5 convolution_convert_fusion.4
  36.7 1.4 fusion.35
  38.6 1.8 broadcast_compare_fusion
  40.3 3.0 copy.131
  44.3 1.1 copy.132
  45.4 23.6 %all-gather = s32[8,1,128]{2,1,0:T(1,128)S(1)} all-gather(s32[1,1,128]{2,1,0:T(1,128)S(1)} %bitcast.259), channel_id=1, replica_groups=mesh['paper'=32,'type'=8] {'type'}, dimensions={0}, use_global_device_ids=true | all-gather | bytes 4608 | tf_op jit(solution)/shard_map/all_gather | solution.py:180
  69.1 1.5 convolution_convert_fusion.2
  70.6 2.2 fusion.34
  72.9 14.2 %all-gather.9.cloned.1.call-done = bf16[1024,1024]{1,0:T(8,128)(2,1)} async-done(((bf16[128,1024]{1,0:T(8,128)(2,1)}), bf16[1024,1024]{1,0:T(8,128)(2,1)}) %all-gather.9.cloned.1.call-update) | async-done | bytes 2097168 | tf_op jit(solution)/shard_map/all_gather | solution.py:174
  87.0 2.7 fusion.100
  89.7 69.1 %all-gather.5.cloned.1.call-done = bf16[4096,512]{0,1:T(8,128)(2,1)} async-done(((bf16[128,512]{0,1:T(8,128)(2,1)}), bf16[4096,512]{0,1:T(8,128)(2,1)}) %all-gather.5.cloned.1.call-update) | async-done | bytes 4194320 | tf_op jit(solution)/shard_map/all_gather | solution.py:165
  158.9 72.7 %all-gather.7.cloned.1.call-done = bf16[4096,512]{0,1:T(8,128)(2,1)} async-done(((bf16[128,512]{0,1:T(8,128)(2,1)}), bf16[4096,512]{0,1:T(8,128)(2,1)}) %all-gather.7.cloned.1.call-update) | async-done | bytes 4194320 | tf_op jit(solution)/shard_map/all_gather | solution.py:164
  231.6 86.4 %while.30 = (s32[]{:T(128)}, f32[512,8,64]{0,2,1:T(8,128)}, f32[512,8]{0,1:T(8,128)S(1)}, bf16[4096,512]{0,1:T(8,128)(2,1)}, pred[512,4096]{1,0:T(8,128)(4,1)}, ...) while((s32[]{:T(128)}, f32[512,8,64]{0,2,1:T(8,128)}, ...), condition=%wide.region_3.4_spmd, body=%wide.region_1.3_spmd.sunk | while | flops 558104576 | bytes 32637168 | solution.py:118
  231.6 1.3 constant_dynamic-slice_fusion.10
  234.3 4.5 %fusion.144 = (f32[8,512]{1,0:T(8,128)S(1)}, f32[8,512,512]{2,1,0:T(8,128)S(1)}) fusion(f32[8,512]{1,0:T(8,128)S(1)} %dynamic-slice_bitcast_fusion.4, pred[512,512]{0,1:T(8,128)(4,1)S(1)} %copy.137, bf16[512,8,64]{0,2,1:T(8,128)(2,1)S(1)} %bitcast.234, bf16[512,8,64]{0,2,1:T(8,128)(2,1)} %get-tuple-element.533), kind=kOutput, calls=%fused_computation.1.clone.1 | convolution fusion | flops 278917120 | bytes 9732096 | tf_op jit(solution)/shard_map/while/body/eval_jaxpr/thd,shd->hts/dot_general | solution.py:86
  238.8 2.6 fusion.145
  242.4 1.3 constant_dynamic-slice_fusion.10
  245.1 4.5 %fusion.144 = (f32[8,512]{1,0:T(8,128)S(1)}, f32[8,512,512]{2,1,0:T(8,128)S(1)}) fusion(f32[8,512]{1,0:T(8,128)S(1)} %dynamic-slice_bitcast_fusion.4, pred[512,512]{0,1:T(8,128)(4,1)S(1)} %copy.137, bf16[512,8,64]{0,2,1:T(8,128)(2,1)S(1)} %bitcast.234, bf16[512,8,64]{0,2,1:T(8,128)(2,1)} %get-tuple-element.533), kind=kOutput, calls=%fused_computation.1.clone.1 | convolution fusion | flops 278917120 | bytes 9732096 | tf_op jit(solution)/shard_map/while/body/eval_jaxpr/thd,shd->hts/dot_general | solution.py:86
  249.6 2.6 fusion.145
  253.2 1.3 constant_dynamic-slice_fusion.10
  255.9 4.5 %fusion.144 = (f32[8,512]{1,0:T(8,128)S(1)}, f32[8,512,512]{2,1,0:T(8,128)S(1)}) fusion(f32[8,512]{1,0:T(8,128)S(1)} %dynamic-slice_bitcast_fusion.4, pred[512,512]{0,1:T(8,128)(4,1)S(1)} %copy.137, bf16[512,8,64]{0,2,1:T(8,128)(2,1)S(1)} %bitcast.234, bf16[512,8,64]{0,2,1:T(8,128)(2,1)} %get-tuple-element.533), kind=kOutput, calls=%fused_computation.1.clone.1 | convolution fusion | flops 278917120 | bytes 9732096 | tf_op jit(solution)/shard_map/while/body/eval_jaxpr/thd,shd->hts/dot_general | solution.py:86
  260.4 2.6 fusion.145
  264.0 1.3 constant_dynamic-slice_fusion.10
  266.7 4.5 %fusion.144 = (f32[8,512]{1,0:T(8,128)S(1)}, f32[8,512,512]{2,1,0:T(8,128)S(1)}) fusion(f32[8,512]{1,0:T(8,128)S(1)} %dynamic-slice_bitcast_fusion.4, pred[512,512]{0,1:T(8,128)(4,1)S(1)} %copy.137, bf16[512,8,64]{0,2,1:T(8,128)(2,1)S(1)} %bitcast.234, bf16[512,8,64]{0,2,1:T(8,128)(2,1)} %get-tuple-element.533), kind=kOutput, calls=%fused_computation.1.clone.1 | convolution fusion | flops 278917120 | bytes 9732096 | tf_op jit(solution)/shard_map/while/body/eval_jaxpr/thd,shd->hts/dot_general | solution.py:86
  271.2 2.6 fusion.145
  274.8 1.3 constant_dynamic-slice_fusion.10
  277.5 4.5 %fusion.144 = (f32[8,512]{1,0:T(8,128)S(1)}, f32[8,512,512]{2,1,0:T(8,128)S(1)}) fusion(f32[8,512]{1,0:T(8,128)S(1)} %dynamic-slice_bitcast_fusion.4, pred[512,512]{0,1:T(8,128)(4,1)S(1)} %copy.137, bf16[512,8,64]{0,2,1:T(8,128)(2,1)S(1)} %bitcast.234, bf16[512,8,64]{0,2,1:T(8,128)(2,1)} %get-tuple-element.533), kind=kOutput, calls=%fused_computation.1.clone.1 | convolution fusion | flops 278917120 | bytes 9732096 | tf_op jit(solution)/shard_map/while/body/eval_jaxpr/thd,shd->hts/dot_general | solution.py:86
  282.0 2.6 fusion.145
  285.6 1.3 constant_dynamic-slice_fusion.10
  288.3 4.5 %fusion.144 = (f32[8,512]{1,0:T(8,128)S(1)}, f32[8,512,512]{2,1,0:T(8,128)S(1)}) fusion(f32[8,512]{1,0:T(8,128)S(1)} %dynamic-slice_bitcast_fusion.4, pred[512,512]{0,1:T(8,128)(4,1)S(1)} %copy.137, bf16[512,8,64]{0,2,1:T(8,128)(2,1)S(1)} %bitcast.234, bf16[512,8,64]{0,2,1:T(8,128)(2,1)} %get-tuple-element.533), kind=kOutput, calls=%fused_computation.1.clone.1 | convolution fusion | flops 278917120 | bytes 9732096 | tf_op jit(solution)/shard_map/while/body/eval_jaxpr/thd,shd->hts/dot_general | solution.py:86
  292.8 2.6 fusion.145
  296.4 1.3 constant_dynamic-slice_fusion.10
  299.1 4.5 %fusion.144 = (f32[8,512]{1,0:T(8,128)S(1)}, f32[8,512,512]{2,1,0:T(8,128)S(1)}) fusion(f32[8,512]{1,0:T(8,128)S(1)} %dynamic-slice_bitcast_fusion.4, pred[512,512]{0,1:T(8,128)(4,1)S(1)} %copy.137, bf16[512,8,64]{0,2,1:T(8,128)(2,1)S(1)} %bitcast.234, bf16[512,8,64]{0,2,1:T(8,128)(2,1)} %get-tuple-element.533), kind=kOutput, calls=%fused_computation.1.clone.1 | convolution fusion | flops 278917120 | bytes 9732096 | tf_op jit(solution)/shard_map/while/body/eval_jaxpr/thd,shd->hts/dot_general | solution.py:86
  303.6 2.6 fusion.145
  307.2 1.3 constant_dynamic-slice_fusion.10
  309.9 4.5 %fusion.144 = (f32[8,512]{1,0:T(8,128)S(1)}, f32[8,512,512]{2,1,0:T(8,128)S(1)}) fusion(f32[8,512]{1,0:T(8,128)S(1)} %dynamic-slice_bitcast_fusion.4, pred[512,512]{0,1:T(8,128)(4,1)S(1)} %copy.137, bf16[512,8,64]{0,2,1:T(8,128)(2,1)S(1)} %bitcast.234, bf16[512,8,64]{0,2,1:T(8,128)(2,1)} %get-tuple-element.533), kind=kOutput, calls=%fused_computation.1.clone.1 | convolution fusion | flops 278917120 | bytes 9732096 | tf_op jit(solution)/shard_map/while/body/eval_jaxpr/thd,shd->hts/dot_general | solution.py:86
  314.4 2.6 fusion.145
  318.0 22.2 %while.31 = (s32[]{:T(128)}, f32[512,8,64]{0,2,1:T(8,128)}, f32[512,8]{0,1:T(8,128)S(1)}, bf16[1024,512]{1,0:T(8,128)(2,1)}, pred[512,1024]{1,0:T(8,128)(4,1)}, ...) while((s32[]{:T(128)}, f32[512,8,64]{0,2,1:T(8,128)}, ...), condition=%wide.region_6.7_spmd, body=%wide.region_4.6_spmd.sunk | while | flops 558104576 | bytes 34734320 | solution.py:118
  318.0 1.1 constant_dynamic-slice_fusion.12
  321.0 4.4 %fusion.150 = (f32[8,512]{1,0:T(8,128)S(1)}, f32[8,512,512]{2,1,0:T(8,128)S(1)}) fusion(f32[8,512]{1,0:T(8,128)S(1)} %dynamic-slice_bitcast_fusion.5, pred[512,512]{0,1:T(8,128)(4,1)S(1)} %copy.139, bf16[512,8,64]{0,2,1:T(8,128)(2,1)S(1)} %bitcast.236, bf16[512,8,64]{0,2,1:T(8,128)(2,1)} %get-tuple-element.569), kind=kOutput, calls=%fused_computation.16.clone.1 | convolution fusion | flops 278917120 | bytes 9732096 | tf_op jit(solution)/shard_map/while/body/eval_jaxpr/thd,shd->hts/dot_general | solution.py:86
  325.5 2.6 fusion.151
  329.1 1.1 constant_dynamic-slice_fusion.12
  332.1 4.5 %fusion.150 = (f32[8,512]{1,0:T(8,128)S(1)}, f32[8,512,512]{2,1,0:T(8,128)S(1)}) fusion(f32[8,512]{1,0:T(8,128)S(1)} %dynamic-slice_bitcast_fusion.5, pred[512,512]{0,1:T(8,128)(4,1)S(1)} %copy.139, bf16[512,8,64]{0,2,1:T(8,128)(2,1)S(1)} %bitcast.236, bf16[512,8,64]{0,2,1:T(8,128)(2,1)} %get-tuple-element.569), kind=kOutput, calls=%fused_computation.16.clone.1 | convolution fusion | flops 278917120 | bytes 9732096 | tf_op jit(solution)/shard_map/while/body/eval_jaxpr/thd,shd->hts/dot_general | solution.py:86
  336.5 2.6 fusion.151
  340.2 3.4 fusion.40
  343.6 1.6 fusion.101
  345.5 1.0 copy.106
  (139 shorter events, 29.5 us)
Async XLA Ops:
  6.5 337.1 %copy-start = (bf16[512,512]{1,0:T(8,128)(2,1)S(1)}, bf16[512,512]{1,0:T(8,128)(2,1)}, u32[]{:S(2)}) copy-start(bf16[512,512]{1,0:T(8,128)(2,1)} %param.33) | copy-start | bytes 1572868
  6.5 25.4 %copy-start.6 = (bf16[512,512]{1,0:T(8,128)(2,1)S(1)}, bf16[512,512]{1,0:T(8,128)(2,1)}, u32[]{:S(2)}) copy-start(bf16[512,512]{1,0:T(8,128)(2,1)} %param.23) | copy-start | bytes 1572868
  6.5 80.5 %all-gather.9.cloned.1.call-start = ((), (), s32[]{:S(2)}) async-start(), calls=%async_computation.2 | async-start | bytes 2359296 | tf_op jit(solution)/shard_map/all_gather | solution.py:174
  7.3 30.9 %copy-start.11 = (f32[4,8]{1,0:T(4,128)S(1)}, f32[4,8]{1,0:T(4,128)}, u32[]{:S(2)}) copy-start(f32[4,8]{1,0:T(4,128)} %param.32) | copy-start | bytes 388
  7.3 31.0 %copy-start.7 = (s32[4,8,128,128]{3,2,1,0:T(8,128)S(1)}, s32[4,8,128,128]{3,2,1,0:T(8,128)}, u32[]{:S(2)}) copy-start(s32[4,8,128,128]{3,2,1,0:T(8,128)} %param.36) | copy-start | bytes 6291460
  13.9 24.6 %copy-start.10 = (s32[4,8]{1,0:T(4,128)S(1)}, s32[4,8]{1,0:T(4,128)}, u32[]{:S(2)}) copy-start(s32[4,8]{1,0:T(4,128)} %param.38) | copy-start | bytes 388
  13.9 24.6 %copy-start.14 = (s32[4,8]{1,0:T(4,128)S(1)}, s32[4,8]{1,0:T(4,128)}, u32[]{:S(2)}) copy-start(s32[4,8]{1,0:T(4,128)} %param.37) | copy-start | bytes 388
  25.2 133.6 %all-gather.5.cloned.1.call-start = ((), (), s32[]{:S(2)}) async-start(), calls=%async_computation | async-start | bytes 4325376 | tf_op jit(solution)/shard_map/all_gather | solution.py:165
  28.6 203.0 %all-gather.7.cloned.1.call-start = ((), (), s32[]{:S(2)}) async-start(), calls=%async_computation.1 | async-start | bytes 4325376 | tf_op jit(solution)/shard_map/all_gather | solution.py:164
  36.7 1.4 copy-start.5
  38.5 4.8 %copy-start.8 = (s32[4,2,128,128]{3,2,1,0:T(8,128)S(1)}, s32[4,2,128,128]{3,2,1,0:T(8,128)}, u32[]{:S(2)}) copy-start(s32[4,2,128,128]{3,2,1,0:T(8,128)} %param.39) | copy-start | bytes 1572868
  38.5 4.9 %copy-start.15 = (s32[4,2]{0,1:T(2,128)S(1)}, s32[4,2]{0,1:T(2,128)}, u32[]{:S(2)}) copy-start(s32[4,2]{0,1:T(2,128)} %param.41) | copy-start | bytes 100
  38.5 5.0 %copy-start.12 = (s32[4,2]{0,1:T(2,128)S(1)}, s32[4,2]{0,1:T(2,128)}, u32[]{:S(2)}) copy-start(s32[4,2]{0,1:T(2,128)} %param.40) | copy-start | bytes 100
  40.3 5.0 %copy-start.13 = (s32[128]{0:T(128)S(1)}, s32[128]{0:T(128)}, u32[]{:S(2)}) copy-start(s32[128]{0:T(128)} %param.26) | copy-start | bytes 1540
  234.3 4.5 %copy-start.1 = (f32[512,8,64]{0,2,1:T(8,128)S(1)}, f32[512,8,64]{0,2,1:T(8,128)}, u32[]{:S(2)}) copy-start(f32[512,8,64]{0,2,1:T(8,128)} %get-tuple-element.516) | copy-start | bytes 3145732 | tf_op jit(solution)/shard_map/while
  241.5 1.0 copy-start.2
  245.1 4.5 %copy-start.1 = (f32[512,8,64]{0,2,1:T(8,128)S(1)}, f32[512,8,64]{0,2,1:T(8,128)}, u32[]{:S(2)}) copy-start(f32[512,8,64]{0,2,1:T(8,128)} %get-tuple-element.516) | copy-start | bytes 3145732 | tf_op jit(solution)/shard_map/while
  252.2 1.0 copy-start.2
  255.9 4.5 %copy-start.1 = (f32[512,8,64]{0,2,1:T(8,128)S(1)}, f32[512,8,64]{0,2,1:T(8,128)}, u32[]{:S(2)}) copy-start(f32[512,8,64]{0,2,1:T(8,128)} %get-tuple-element.516) | copy-start | bytes 3145732 | tf_op jit(solution)/shard_map/while
  263.0 1.0 copy-start.2
  266.7 4.5 %copy-start.1 = (f32[512,8,64]{0,2,1:T(8,128)S(1)}, f32[512,8,64]{0,2,1:T(8,128)}, u32[]{:S(2)}) copy-start(f32[512,8,64]{0,2,1:T(8,128)} %get-tuple-element.516) | copy-start | bytes 3145732 | tf_op jit(solution)/shard_map/while
  273.8 1.0 copy-start.2
  277.5 4.5 %copy-start.1 = (f32[512,8,64]{0,2,1:T(8,128)S(1)}, f32[512,8,64]{0,2,1:T(8,128)}, u32[]{:S(2)}) copy-start(f32[512,8,64]{0,2,1:T(8,128)} %get-tuple-element.516) | copy-start | bytes 3145732 | tf_op jit(solution)/shard_map/while
  284.6 1.0 copy-start.2
  288.3 4.5 %copy-start.1 = (f32[512,8,64]{0,2,1:T(8,128)S(1)}, f32[512,8,64]{0,2,1:T(8,128)}, u32[]{:S(2)}) copy-start(f32[512,8,64]{0,2,1:T(8,128)} %get-tuple-element.516) | copy-start | bytes 3145732 | tf_op jit(solution)/shard_map/while
  295.4 1.0 copy-start.2
  299.1 4.5 %copy-start.1 = (f32[512,8,64]{0,2,1:T(8,128)S(1)}, f32[512,8,64]{0,2,1:T(8,128)}, u32[]{:S(2)}) copy-start(f32[512,8,64]{0,2,1:T(8,128)} %get-tuple-element.516) | copy-start | bytes 3145732 | tf_op jit(solution)/shard_map/while
  306.2 1.0 copy-start.2
  309.9 4.5 %copy-start.1 = (f32[512,8,64]{0,2,1:T(8,128)S(1)}, f32[512,8,64]{0,2,1:T(8,128)}, u32[]{:S(2)}) copy-start(f32[512,8,64]{0,2,1:T(8,128)} %get-tuple-element.516) | copy-start | bytes 3145732 | tf_op jit(solution)/shard_map/while
  317.0 1.0 copy-start.2
  318.0 27.4 %copy-start.9 = (f32[512]{0:T(512)S(1)}, f32[512]{0:T(512)}, u32[]{:S(2)}) copy-start(f32[512]{0:T(512)} %param.35) | copy-start | bytes 6148
  321.0 4.5 %copy-start.3 = (f32[512,8,64]{0,2,1:T(8,128)S(1)}, f32[512,8,64]{0,2,1:T(8,128)}, u32[]{:S(2)}) copy-start(f32[512,8,64]{0,2,1:T(8,128)} %get-tuple-element.552) | copy-start | bytes 3145732 | tf_op jit(solution)/shard_map/while
  328.1 1.0 copy-start.4
  332.1 4.5 %copy-start.3 = (f32[512,8,64]{0,2,1:T(8,128)S(1)}, f32[512,8,64]{0,2,1:T(8,128)}, u32[]{:S(2)}) copy-start(f32[512,8,64]{0,2,1:T(8,128)} %get-tuple-element.552) | copy-start | bytes 3145732 | tf_op jit(solution)/shard_map/while
  339.2 1.0 copy-start.4
Sparse Core Ops, SparseCore 0:
  25.4 61.6 all-gather.8
  88.8 70.0 all-gather.4
  160.7 70.8 all-gather.6
